TPU v7x, 256 devices: a whole 4x4x8 slice. The times are simulated.
256 devices in a mesh: dp: 32 (over x, y, core), mp: 8 (over z).
Axes of the slice: x: 4, y: 4, z: 8, core: 2. Of those that a mesh axis runs over, the one named last changes fastest.
Arguments:
- context: bfloat16 [16384, 4096], P('dp', 'mp'), may hold values from -16 to 16
- upstream: bfloat16 [16384, 4096], P('dp'), may hold values from -8 to 8
- out_proj: bfloat16 [4096, 4096], P('mp'), may hold values from -0.09375 to 0.09375
Outputs:
- combined_grad: bfloat16 [4096, 4096], P('mp')
- context_grad: bfloat16 [16384, 4096], P('dp', 'mp')
All inputs are finite; a program needn't handle non-finite values.
Results may differ from a plain program's by a relative error of at most 0.001.
The roundings to bfloat16 on the way count: a program that leaves them out, or rounds other values in their place, can miss the bound.
Values may be sent and summed in bfloat16 or wider, within the bound.
A program may use at most 64 MiB of HBM per device.

v0:
```python
import math

import jax
import jax.numpy as jnp
from jax import lax
from jax.sharding import PartitionSpec as P

EPSILON = 1e-06


def partner_2(value, axis, stride):
    return lax.ppermute(value, axis, [(i, i ^ 1 << stride) for i in range(lax.axis_size(axis))])


def mix_pair(left, right, crossed, left_norm, right_norm):
    left_wide = left.astype(jnp.float32)
    right_wide = right.astype(jnp.float32)
    mixed = (1.0 - crossed / (2.0 * (left_norm + EPSILON))) * left_wide + (
        1.0 - crossed / (2.0 * (right_norm + EPSILON))
    ) * right_wide
    return mixed.astype(jnp.bfloat16)


def partial_terms(left, right):
    left_wide = left.astype(jnp.float32)
    right_wide = right.astype(jnp.float32)
    return jnp.stack(
        [
            jnp.sum(left_wide * right_wide),
            jnp.sum(left_wide * left_wide),
            jnp.sum(right_wide * right_wide),
        ]
    )


def shards(context, upstream, out_proj):
    scaling = 1.0 / math.sqrt(context.shape[0])
    local_grad = lax.dot_general(
        context, upstream, (((0,), (0,)), ((), ())), preferred_element_type=jnp.float32
    )
    local_grad = (local_grad * scaling).astype(jnp.bfloat16)
    context_grad = lax.dot_general(
        upstream, out_proj, (((1,), (1,)), ((), ())), preferred_element_type=jnp.float32
    ).astype(jnp.bfloat16)
    replicas = lax.axis_size("dp")
    levels = replicas.bit_length() - 1
    index = lax.axis_index("dp")
    row_block = local_grad.shape[0] // replicas
    width = local_grad.shape[1]
    current = local_grad.reshape(replicas, row_block, width)
    for level in range(levels):
        blocks = current.shape[0]
        paired = current.reshape(blocks // 2, 2, row_block, width)
        bit_value = index >> level & 1
        kept = lax.dynamic_index_in_dim(paired, bit_value, 1, keepdims=False)
        sent = lax.dynamic_index_in_dim(paired, 1 - bit_value, 1, keepdims=False)
        partner = partner_2(sent, "dp", level)
        lower = bit_value == 0
        left = jnp.where(lower, kept, partner)
        right = jnp.where(lower, partner, kept)
        terms = partial_terms(left, right)
        sums = lax.psum(terms, "mp")
        for section in range(level + 1):
            other = partner_2(sums, "dp", section)
            sums = sums + other
        current = mix_pair(left, right, sums[0], sums[1], sums[2])
    combined = lax.all_gather(current.reshape(row_block, width), "dp", axis=0, tiled=True)
    return (combined, context_grad)


def solution(mesh):
    in_specs = (P("dp", "mp"), P("dp", None), P("mp", None))
    out_specs = (P("mp", None), P("dp", "mp"))
    return jax.shard_map(shards, mesh=mesh, in_specs=in_specs, out_specs=out_specs, check_vma=False)
```

profile of v0, /device:TPU:1, one launch (start us, length us, event | category | flops | bytes accessed | tf_op | source)
XLA Modules:
  0.0 307.1 jit_solution(5900115934543127904)
XLA Ops:
  8.2 4.6 %multiply_convert_fusion = bf16[512,4096]{1,0:T(8,128)(2,1)S(1)} fusion(bf16[512,512]{1,0:T(8,128)(2,1)S(1)} %copy-done, bf16[512,4096]{1,0:T(8,128)(2,1)} %param.4), kind=kOutput, calls=%fused_computation | convolution fusion | flops 2151677952 | bytes 8912896 | tf_op jit(solution)/shard_map/dot_general | solution.py:38
  14.9 3.3 %collective-permute-start = (bf16[16,16,4096]{2,1,0:T(8,128)(2,1)S(1)}, bf16[16,16,4096]{2,1,0:T(8,128)(2,1)}, u32[]{:S(2)}, u32[]{:S(2)}) collective-permute-start(bf16[16,16,4096]{2,1,0:T(8,128)(2,1)S(1)} %dynamic-slice_bitcast_fusion), channel_id=1, source_target_pairs={{0,8},{8,0},{16,24},{24,16},{32,40},{40,32},{48,56},{56,48},{64,72... | collective-permute-start | bytes 6291464 | tf_op jit(solution)/shard_map/ppermute | solution.py:12
  18.3 3.9 %collective-permute-done = bf16[16,16,4096]{2,1,0:T(8,128)(2,1)} collective-permute-done((bf16[16,16,4096]{2,1,0:T(8,128)(2,1)S(1)}, bf16[16,16,4096]{2,1,0:T(8,128)(2,1)}, u32[]{:S(2)}, u32[]{:S(2)}) %collective-permute-start) | collective-permute-done | bytes 2097184 | tf_op jit(solution)/shard_map/ppermute | solution.py:12
  22.2 4.7 %fusion.3 = (f32[]{:T(128)}, f32[]{:T(128)}, f32[]{:T(128)}, bf16[16,16,4096]{2,1,0:T(8,128)(2,1)S(1)}, bf16[16,16,4096]{2,1,0:T(8,128)(2,1)}) fusion(bf16[16,16,4096]{2,1,0:T(8,128)(2,1)} %collective-permute-done, bf16[16,2,16,4096]{3,2,1,0:T(8,128)(2,1)} %bitcast.63, s32[]{:T(128)S(6)} %select_n.100, pred[]{:T(512)S(6)} %eq.19), kind=kLoop, calls=%fused_computation.9 | loop fusion | flops 10485757 | bytes 8388625 | tf_op jit(solution)/shard_map/reduce_sum | solution.py:29
  28.9 14.5 %psum.35 = f32[3]{0:T(128)S(1)} all-reduce(f32[3]{0:T(128)S(1)} %pad_maximum_fusion), channel_id=1, replica_groups=mesh['dp'=32,'mp'=8] {'mp'}, use_global_device_ids=true, to_apply=%region_3.4 | all-reduce | flops 3 | bytes 24 | tf_op jit(solution)/shard_map/psum | solution.py:62
  43.3 4.2 %collective-permute-start.1 = (f32[3]{0:T(128)S(1)}, f32[3]{0:T(128)S(1)}, u32[]{:S(2)}, u32[]{:S(2)}) collective-permute-start(f32[3]{0:T(128)S(1)} %psum.35), channel_id=1, source_target_pairs={{0,8},{8,0},{16,24},{24,16},{32,40},{40,32},{48,56},{56,48},{64,72... | collective-permute-start | bytes 44 | tf_op jit(solution)/shard_map/ppermute | solution.py:12
  51.5 2.4 fusion.2
  56.7 23.3 %collective-permute-done.2 = bf16[8,16,4096]{2,1,0:T(8,128)(2,1)} collective-permute-done((bf16[8,16,4096]{2,1,0:T(8,128)(2,1)S(1)}, bf16[8,16,4096]{2,1,0:T(8,128)(2,1)}, u32[]{:S(2)}, u32[]{:S(2)}) %collective-permute-start.2) | collective-permute-done | bytes 1048608 | tf_op jit(solution)/shard_map/ppermute | solution.py:12
  80.0 3.0 fusion.8
  84.9 10.7 %psum.36 = f32[3]{0:T(128)S(1)} all-reduce(f32[3]{0:T(128)S(1)} %pad_maximum_fusion.1), channel_id=1, replica_groups=mesh['dp'=32,'mp'=8] {'mp'}, use_global_device_ids=true, to_apply=%region_7.8 | all-reduce | flops 3 | bytes 24 | tf_op jit(solution)/shard_map/psum | solution.py:62
  95.6 4.7 %collective-permute-start.3 = (f32[3]{0:T(128)S(1)}, f32[3]{0:T(128)S(1)}, u32[]{:S(2)}, u32[]{:S(2)}) collective-permute-start(f32[3]{0:T(128)S(1)} %psum.36), channel_id=1, source_target_pairs={{0,8},{8,0},{16,24},{24,16},{32,40},{40,32},{48,56},{56,48},{64,72... | collective-permute-start | bytes 44 | tf_op jit(solution)/shard_map/ppermute | solution.py:12
  108.3 3.0 collective-permute-start.5
  111.3 10.6 %collective-permute-done.5 = bf16[4,16,4096]{2,1,0:T(8,128)(2,1)S(1)} collective-permute-done((bf16[4,16,4096]{2,1,0:T(8,128)(2,1)S(1)}, bf16[4,16,4096]{2,1,0:T(8,128)(2,1)S(1)}, u32[]{:S(2)}, u32[]{:S(2)}) %collective-permute-start.5) | collective-permute-done | bytes 524320 | tf_op jit(solution)/shard_map/ppermute | solution.py:12
  121.8 2.1 fusion.13
  125.9 12.4 %psum.37 = f32[3]{0:T(128)S(1)} all-reduce(f32[3]{0:T(128)S(1)} %pad_maximum_fusion.2), channel_id=1, replica_groups=mesh['dp'=32,'mp'=8] {'mp'}, use_global_device_ids=true, to_apply=%region_11.12 | all-reduce | flops 3 | bytes 24 | tf_op jit(solution)/shard_map/psum | solution.py:62
  138.3 6.2 %collective-permute-start.6 = (f32[3]{0:T(128)S(1)}, f32[3]{0:T(128)S(1)}, u32[]{:S(2)}, u32[]{:S(2)}) collective-permute-start(f32[3]{0:T(128)S(1)} %psum.37), channel_id=1, source_target_pairs={{0,8},{8,0},{16,24},{24,16},{32,40},{40,32},{48,56},{56,48},{64,72... | collective-permute-start | bytes 44 | tf_op jit(solution)/shard_map/ppermute | solution.py:12
  147.7 2.9 collective-permute-start.8
  156.7 4.0 %collective-permute-done.9 = bf16[2,16,4096]{2,1,0:T(8,128)(2,1)S(1)} collective-permute-done((bf16[2,16,4096]{2,1,0:T(8,128)(2,1)S(1)}, bf16[2,16,4096]{2,1,0:T(8,128)(2,1)S(1)}, u32[]{:S(2)}, u32[]{:S(2)}) %collective-permute-start.9) | collective-permute-done | bytes 262176 | tf_op jit(solution)/shard_map/ppermute | solution.py:12
  161.6 2.1 pad_maximum_fusion.3
  163.7 10.7 %psum.38 = f32[3]{0:T(128)S(1)} all-reduce(f32[3]{0:T(128)S(1)} %pad_maximum_fusion.3), channel_id=1, replica_groups=mesh['dp'=32,'mp'=8] {'mp'}, use_global_device_ids=true, to_apply=%region_15.16 | all-reduce | flops 3 | bytes 24 | tf_op jit(solution)/shard_map/psum | solution.py:62
  174.3 7.3 %collective-permute-start.10 = (f32[3]{0:T(128)S(1)}, f32[3]{0:T(128)S(1)}, u32[]{:S(2)}, u32[]{:S(2)}) collective-permute-start(f32[3]{0:T(128)S(1)} %psum.38), channel_id=1, source_target_pairs={{0,8},{8,0},{16,24},{24,16},{32,40},{40,32},{48,56},{56,48},{64,72... | collective-permute-start | bytes 44 | tf_op jit(solution)/shard_map/ppermute | solution.py:12
  184.8 2.9 collective-permute-start.12
  194.6 2.8 collective-permute-start.14
  197.5 2.6 collective-permute-done.14
  200.8 2.1 pad_maximum_fusion.4
  202.9 12.4 %psum.39 = f32[3]{0:T(128)S(1)} all-reduce(f32[3]{0:T(128)S(1)} %pad_maximum_fusion.4), channel_id=1, replica_groups=mesh['dp'=32,'mp'=8] {'mp'}, use_global_device_ids=true, to_apply=%region_19.20 | all-reduce | flops 3 | bytes 24 | tf_op jit(solution)/shard_map/psum | solution.py:62
  215.3 8.7 %collective-permute-start.15 = (f32[3]{0:T(128)S(1)}, f32[3]{0:T(128)S(1)}, u32[]{:S(2)}, u32[]{:S(2)}) collective-permute-start(f32[3]{0:T(128)S(1)} %psum.39), channel_id=1, source_target_pairs={{0,8},{8,0},{16,24},{24,16},{32,40},{40,32},{48,56},{56,48},{64,72... | collective-permute-start | bytes 44 | tf_op jit(solution)/shard_map/ppermute | solution.py:12
  227.2 2.9 collective-permute-start.17
  233.5 2.7 collective-permute-start.19
  241.5 6.6 %convolution_convert_fusion = bf16[512,512]{1,0:T(8,128)(2,1)} fusion(bf16[512,4096]{1,0:T(8,128)(2,1)} %param.4, bf16[512,4096]{1,0:T(8,128)(2,1)} %param.5), kind=kOutput, calls=%fused_computation.29 | convolution fusion | flops 2147745792 | bytes 8912896 | tf_op jit(solution)/shard_map/dot_general | solution.py:42
  248.1 47.4 %all-gather.3.cloned.1.call-done = bf16[1,512,4096]{2,1,0:T(8,128)(2,1)} async-done(((bf16[1,16,4096]{2,1,0:T(8,128)(2,1)}), bf16[1,512,4096]{2,1,0:T(8,128)(2,1)}) %all-gather.3.cloned.1.call-update) | async-done | bytes 4194320 | tf_op jit(solution)/shard_map/all_gather | solution.py:67
  295.6 4.7 %copy.6 = bf16[512,4096]{1,0:T(8,128)(2,1)} copy(bf16[512,4096]{1,0:T(8,128)(2,1)} %bitcast.66) | data formatting | bytes 8388608
  (67 shorter events, 43.3 us)
Async XLA Ops:
  7.2 1.0 copy-start
  7.2 288.4 %all-gather.3.cloned.1.call-start = ((), (), s32[]{:S(2)}) async-start(), calls=%async_computation | async-start | bytes 4325376 | tf_op jit(solution)/shard_map/all_gather | solution.py:67
  12.8 2.0 copy-start.1
  14.9 7.2 %collective-permute-start = (bf16[16,16,4096]{2,1,0:T(8,128)(2,1)S(1)}, bf16[16,16,4096]{2,1,0:T(8,128)(2,1)}, u32[]{:S(2)}, u32[]{:S(2)}) collective-permute-start(bf16[16,16,4096]{2,1,0:T(8,128)(2,1)S(1)} %dynamic-slice_bitcast_fusion), channel_id=1, source_target_pairs={{0,8},{8,0},{16,24},{24,16},{32,40},{40,32},{48,56},{56,48},{64,72... | collective-permute-start | bytes 6291464 | tf_op jit(solution)/shard_map/ppermute | solution.py:12
  43.3 5.0 %collective-permute-start.1 = (f32[3]{0:T(128)S(1)}, f32[3]{0:T(128)S(1)}, u32[]{:S(2)}, u32[]{:S(2)}) collective-permute-start(f32[3]{0:T(128)S(1)} %psum.35), channel_id=1, source_target_pairs={{0,8},{8,0},{16,24},{24,16},{32,40},{40,32},{48,56},{56,48},{64,72... | collective-permute-start | bytes 44 | tf_op jit(solution)/shard_map/ppermute | solution.py:12
  53.9 1.3 copy-start.2
  55.3 24.6 %collective-permute-start.2 = (bf16[8,16,4096]{2,1,0:T(8,128)(2,1)S(1)}, bf16[8,16,4096]{2,1,0:T(8,128)(2,1)}, u32[]{:S(2)}, u32[]{:S(2)}) collective-permute-start(bf16[8,16,4096]{2,1,0:T(8,128)(2,1)S(1)} %dynamic-slice_bitcast_fusion.1), channel_id=1, source_target_pairs={{0,16},{8,24},{16,0},{24,8},{32,48},{40,56},{48,32},{56,40},{64,80... | collective-permute-start | bytes 3145736 | tf_op jit(solution)/shard_map/ppermute | solution.py:12
  95.6 5.5 %collective-permute-start.3 = (f32[3]{0:T(128)S(1)}, f32[3]{0:T(128)S(1)}, u32[]{:S(2)}, u32[]{:S(2)}) collective-permute-start(f32[3]{0:T(128)S(1)} %psum.36), channel_id=1, source_target_pairs={{0,8},{8,0},{16,24},{24,16},{32,40},{40,32},{48,56},{56,48},{64,72... | collective-permute-start | bytes 44 | tf_op jit(solution)/shard_map/ppermute | solution.py:12
  101.1 2.4 collective-permute-start.4
  107.2 1.0 copy-start.3
  108.3 13.6 %collective-permute-start.5 = (bf16[4,16,4096]{2,1,0:T(8,128)(2,1)S(1)}, bf16[4,16,4096]{2,1,0:T(8,128)(2,1)S(1)}, u32[]{:S(2)}, u32[]{:S(2)}) collective-permute-start(bf16[4,16,4096]{2,1,0:T(8,128)(2,1)S(1)} %dynamic-slice_bitcast_fusion.2), channel_id=1, source_target_pairs={{0,32},{8,40},{16,48},{24,56},{32,0},{40,8},{48,16},{56,24},{64,96... | collective-permute-start | bytes 1572872 | tf_op jit(solution)/shard_map/ppermute | solution.py:12
  138.3 7.0 %collective-permute-start.6 = (f32[3]{0:T(128)S(1)}, f32[3]{0:T(128)S(1)}, u32[]{:S(2)}, u32[]{:S(2)}) collective-permute-start(f32[3]{0:T(128)S(1)} %psum.37), channel_id=1, source_target_pairs={{0,8},{8,0},{16,24},{24,16},{32,40},{40,32},{48,56},{56,48},{64,72... | collective-permute-start | bytes 44 | tf_op jit(solution)/shard_map/ppermute | solution.py:12
  145.3 2.4 collective-permute-start.7
  147.7 3.9 %collective-permute-start.8 = (f32[3]{0:T(128)S(1)}, f32[3]{0:T(128)S(1)}, u32[]{:S(2)}, u32[]{:S(2)}) collective-permute-start(f32[3]{0:T(128)S(1)} %add.166), channel_id=1, source_target_pairs={{0,32},{8,40},{16,48},{24,56},{32,0},{40,8},{48,16},{56,24},{64,96... | collective-permute-start | bytes 44 | tf_op jit(solution)/shard_map/ppermute | solution.py:12
  155.2 5.5 %collective-permute-start.9 = (bf16[2,16,4096]{2,1,0:T(8,128)(2,1)S(1)}, bf16[2,16,4096]{2,1,0:T(8,128)(2,1)S(1)}, u32[]{:S(2)}, u32[]{:S(2)}) collective-permute-start(bf16[2,16,4096]{2,1,0:T(8,128)(2,1)S(1)} %dynamic-slice_bitcast_fusion.3), channel_id=1, source_target_pairs={{0,64},{8,72},{16,80},{24,88},{32,96},{40,104},{48,112},{56,120},{... | collective-permute-start | bytes 786440 | tf_op jit(solution)/shard_map/ppermute | solution.py:12
  174.3 8.1 %collective-permute-start.10 = (f32[3]{0:T(128)S(1)}, f32[3]{0:T(128)S(1)}, u32[]{:S(2)}, u32[]{:S(2)}) collective-permute-start(f32[3]{0:T(128)S(1)} %psum.38), channel_id=1, source_target_pairs={{0,8},{8,0},{16,24},{24,16},{32,40},{40,32},{48,56},{56,48},{64,72... | collective-permute-start | bytes 44 | tf_op jit(solution)/shard_map/ppermute | solution.py:12
  182.4 2.4 collective-permute-start.11
  184.8 3.9 %collective-permute-start.12 = (f32[3]{0:T(128)S(1)}, f32[3]{0:T(128)S(1)}, u32[]{:S(2)}, u32[]{:S(2)}) collective-permute-start(f32[3]{0:T(128)S(1)} %add.174), channel_id=1, source_target_pairs={{0,32},{8,40},{16,48},{24,56},{32,0},{40,8},{48,16},{56,24},{64,96... | collective-permute-start | bytes 44 | tf_op jit(solution)/shard_map/ppermute | solution.py:12
  188.7 2.4 collective-permute-start.13
  194.6 5.4 %collective-permute-start.14 = (bf16[1,16,4096]{2,1,0:T(8,128)(2,1)S(1)}, bf16[1,16,4096]{2,1,0:T(8,128)(2,1)S(1)}, u32[]{:S(2)}, u32[]{:S(2)}) collective-permute-start(bf16[1,16,4096]{2,1,0:T(8,128)(2,1)S(1)} %constant_dynamic-slice_fusion), channel_id=1, source_target_pairs={{0,128},{8,136},{16,144},{24,152},{32,160},{40,168},{48,176},{56,1... | collective-permute-start | bytes 393224 | tf_op jit(solution)/shard_map/ppermute | solution.py:12
  215.3 9.5 %collective-permute-start.15 = (f32[3]{0:T(128)S(1)}, f32[3]{0:T(128)S(1)}, u32[]{:S(2)}, u32[]{:S(2)}) collective-permute-start(f32[3]{0:T(128)S(1)} %psum.39), channel_id=1, source_target_pairs={{0,8},{8,0},{16,24},{24,16},{32,40},{40,32},{48,56},{56,48},{64,72... | collective-permute-start | bytes 44 | tf_op jit(solution)/shard_map/ppermute | solution.py:12
  224.8 2.4 collective-permute-start.16
  227.2 3.9 %collective-permute-start.17 = (f32[3]{0:T(128)S(1)}, f32[3]{0:T(128)S(1)}, u32[]{:S(2)}, u32[]{:S(2)}) collective-permute-start(f32[3]{0:T(128)S(1)} %add.183), channel_id=1, source_target_pairs={{0,32},{8,40},{16,48},{24,56},{32,0},{40,8},{48,16},{56,24},{64,96... | collective-permute-start | bytes 44 | tf_op jit(solution)/shard_map/ppermute | solution.py:12
  231.1 2.4 collective-permute-start.18
  233.5 3.9 %collective-permute-start.19 = (f32[3]{0:T(128)S(1)}, f32[3]{0:T(128)S(1)}, u32[]{:S(2)}, u32[]{:S(2)}) collective-permute-start(f32[3]{0:T(128)S(1)} %add.185), channel_id=1, source_target_pairs={{0,128},{8,136},{16,144},{24,152},{32,160},{40,168},{48,176},{56,1... | collective-permute-start | bytes 44 | tf_op jit(solution)/shard_map/ppermute | solution.py:12
Sparse Core Ops, SparseCore 0:
  241.6 53.8 all-gather.2
where the time goes:
time: 308 us; the launch traced here: 307 us
  waiting for transfers between devices  107 us (35%)
  starting transfers between devices  62.3 us (20%)
  blocking collectives  60.6 us (20%)
  between operations  27.5 us (9%)
  other arithmetic  25.3 us (8%)
  local copies, waits for them, and re-layouts  13.5 us (4%)
  matrix products  11.2 us (4%)
    ppermute x20, starting transfers between devices, partner_2(): lax.ppermute(value, axis, [(i, i ^ 1 << stride) for i in range(lax.axis_s...  62.3 us
    psum x5, blocking collectives, shards(): sums = lax.psum(terms, 'mp')  60.6 us
    ppermute x20, waiting for transfers between devices, partner_2(): lax.ppermute(value, axis, [(i, i ^ 1 << stride) for i in range(lax.axis_s...  59.2 us
    all_gather x1, waiting for transfers between devices, shards(): lax.all_gather(current.reshape(row_block, width), 'dp', axis=0, tiled=True)  47.4 us
    reduce_sum x5, other arithmetic, partial_terms(): jnp.sum(left_wide * right_wide)  11.5 us
    another operation x5, other arithmetic, partial_terms(): jnp.stack([jnp.sum(left_wide * right_wide), jnp.sum(left_wide * left_wide...  9.99 us
    unnamed x9, local copies, waits for them, and re-layouts  9.97 us
    dot_general x1, matrix products, shards(): lax.dot_general(upstream, out_proj, (((1,), (1,)), ((), ())), preferred_e...  6.62 us
  transfers between devices with their start and end apart: 21, of which 21 were waited for; matrix products, arithmetic and copies ran while one was open for 2% of the time, Pallas kernels for 0%

commit v1 on v0

v1 whole, which is shorter than its diff:
```python
import functools
import math

import jax
import jax.numpy as jnp
from jax import lax
from jax.experimental import pallas as pl
from jax.experimental.pallas import tpu as pltpu
from jax.sharding import PartitionSpec as P

EPSILON = 1e-06
MESH = pl.DeviceIdType.MESH
NX, NY, NZ = 4, 4, 8
CHIPS = NX * NY
GROUP = 2 * NZ
TOK = 512
HEADS = 512
HALF = HEADS // 2
ROWS = HALF // CHIPS
WIDTH = 4096
CHUNKS = 8
CW = WIDTH // CHUNKS
PIECES = 4
PW = WIDTH // PIECES
GPIECES = 4
GW = WIDTH // GPIECES


def remote(src, dst, send, recv, device):
    return pltpu.make_async_remote_copy(
        src_ref=src, dst_ref=dst, send_sem=send, recv_sem=recv, device_id=device, device_id_type=MESH
    )


def kernel(
    ctx_hbm, up_hbm, proj_hbm, comb, cgv,
    ctx_own, ctx_sib, up, proj, left_t, sent, own, par, got,
    block, blocks, gram, gblock, gblocks, pblock, pblocks, weights,
    load_sem, up_sem, x_send, x_recv, z_send, z_recv, a_send, a_recv,
    g_send, g_recv, p_send, p_recv, r_send, r_recv, s_send, s_recv,
):
    dp = lax.axis_index("dp")
    z = lax.axis_index("mp")
    core = lax.rem(dp, 2)
    chip = lax.div(dp, 2)
    x = lax.div(chip, NY)
    y = lax.rem(chip, NY)
    place = z * 2 + core
    sibling = (chip * 2 + 1 - core, z)

    def plane_device(t):
        return (t * 2 + core, z)

    def group_device(g):
        return (chip * 2 + lax.rem(g, 2), lax.div(g, 2))

    def plane_peer(k):
        hi, lo = lax.div(k, 4), lax.rem(k, 4)
        dx = jnp.where(core == 0, hi, lo)
        dy = jnp.where(core == 0, lo, hi)
        return lax.rem(x + dx, NX) * NY + lax.rem(y + dy, NY)

    own_cols = pl.ds(pl.multiple_of(core * HALF, HALF), HALF)
    sib_cols = pl.ds(pl.multiple_of((1 - core) * HALF, HALF), HALF)
    load_sib = pltpu.make_async_copy(ctx_hbm.at[:, sib_cols], ctx_sib, load_sem.at[0])
    load_own = pltpu.make_async_copy(ctx_hbm.at[:, own_cols], ctx_own, load_sem.at[1])
    load_proj = pltpu.make_async_copy(proj_hbm, proj, load_sem.at[2])
    load_sib.start()

    def load_up(i):
        cols = pl.ds(pl.multiple_of(i * CW, CW), CW)
        return pltpu.make_async_copy(up_hbm.at[:, cols], up.at[:, cols], up_sem.at[i])

    for i in range(CHUNKS):
        load_up(i).start()
    load_own.start()
    load_proj.start()

    barrier = pltpu.get_barrier_semaphore()

    def greet_group(k, carry):
        pl.semaphore_signal(barrier, inc=1, device_id=group_device(lax.rem(place + k, GROUP)), device_id_type=MESH)
        return carry

    def greet_plane(k, carry):
        pl.semaphore_signal(barrier, inc=1, device_id=plane_device(plane_peer(k)), device_id_type=MESH)
        return carry

    lax.fori_loop(1, GROUP, greet_group, 0)
    lax.fori_loop(1, CHIPS, greet_plane, 0)

    scaling = 1.0 / math.sqrt(TOK)

    def gradient(out):
        def step(i, carry):
            cols = pl.ds(pl.multiple_of(i * CW, CW), CW)
            product = jnp.dot(left_t[...], up[:, cols], preferred_element_type=jnp.float32)
            out[:, cols] = (product * scaling).astype(jnp.bfloat16)
            return carry
        return step

    load_sib.wait()
    left_t[...] = ctx_sib[...].T
    for i in range(CHUNKS):
        load_up(i).wait()
    lax.fori_loop(0, CHUNKS, gradient(sent), 0)
    pl.semaphore_wait(barrier, GROUP - 1 + CHIPS - 1)

    def exchange(i):
        cols = pl.ds(pl.multiple_of(i * CW, CW), CW)
        return remote(sent.at[:, cols], par.at[:, cols], x_send.at[i], x_recv.at[i], sibling)

    def start_exchange(i, carry):
        exchange(i).start()
        return carry

    lax.fori_loop(0, CHUNKS, start_exchange, 0)
    load_own.wait()
    left_t[...] = ctx_own[...].T
    lax.fori_loop(0, CHUNKS, gradient(own), 0)

    zero = jnp.zeros((8, CW), jnp.float32)

    def chunk_sums(i, sums):
        exchange(i).wait_recv()
        cols = pl.ds(pl.multiple_of(i * CW, CW), CW)

        def rows_sums(r, sums):
            crossed, mine, theirs = sums
            rows = pl.ds(pl.multiple_of(r * 16, 16), 16)
            a = own[rows, cols].astype(jnp.float32)
            b = par[rows, cols].astype(jnp.float32)

            def fold(v):
                return v[:8] + v[8:]

            return crossed + fold(a * b), mine + fold(a * a), theirs + fold(b * b)

        return lax.fori_loop(0, HALF // 16, rows_sums, sums, unroll=2)

    crossed, mine, theirs = lax.fori_loop(0, CHUNKS, chunk_sums, (zero, zero, zero))

    def to_row(v):
        v = jnp.sum(v, axis=0, keepdims=True)
        return sum(v[:, j * 128 : (j + 1) * 128] for j in range(CW // 128))

    crossed, mine, theirs = to_row(crossed), to_row(mine), to_row(theirs)
    first = jnp.where(core == 0, mine, theirs)
    second = jnp.where(core == 0, theirs, mine)
    block[...] = jnp.zeros((8, 128), jnp.float32)
    block[0:1, :] = crossed
    block[1:2, :] = first
    block[2:3, :] = second

    def reduce_over(count, me, peer, src, dst, send, recv):
        dst[me] = src[...]

        def copy(k):
            return remote(src, dst.at[me], send.at[k], recv.at[k], peer(k))

        def start(k, carry):
            copy(k).start()
            return carry

        def wait(k, carry):
            copy(k).wait()
            return carry

        lax.fori_loop(1, count, start, 0)
        lax.fori_loop(1, count, wait, 0)
        total = dst[0]
        for i in range(1, count):
            total = total + dst[i]
        return total

    total = reduce_over(
        GROUP, place, lambda k: group_device(lax.rem(place + k, GROUP)), block, blocks, z_send, z_recv
    )
    total = jnp.sum(total, axis=1, keepdims=True)
    crossed, first, second = total[0:1], total[1:2], total[2:3]
    first_by = 1.0 - crossed / (2.0 * (first + EPSILON))
    second_by = 1.0 - crossed / (2.0 * (second + EPSILON))
    own_by = jnp.where(core == 0, first_by, second_by)
    par_by = jnp.where(core == 0, second_by, first_by)

    def mixed(t, p):
        rows = pl.ds(pl.multiple_of(t * ROWS, ROWS), ROWS)
        cols = pl.ds(pl.multiple_of(p * PW, PW), PW)
        a = own[rows, cols].astype(jnp.float32)
        b = par[rows, cols].astype(jnp.float32)
        return (own_by * a + par_by * b).astype(jnp.bfloat16)

    def spread(k, p):
        t = plane_peer(k)
        rows = pl.ds(pl.multiple_of(t * ROWS, ROWS), ROWS)
        to = pl.ds(pl.multiple_of(chip * ROWS, ROWS), ROWS)
        cols = pl.ds(pl.multiple_of(p * PW, PW), PW)
        return remote(own.at[rows, cols], got.at[to, cols], a_send.at[p, k], a_recv.at[p, k], plane_device(t))

    def mix_piece(p, carry):
        def mix_one(k, carry):
            t = plane_peer(k)
            rows = pl.ds(pl.multiple_of(t * ROWS, ROWS), ROWS)
            cols = pl.ds(pl.multiple_of(p * PW, PW), PW)
            own[rows, cols] = mixed(t, p)
            spread(k, p).start()
            return carry

        lax.fori_loop(1, CHIPS, mix_one, 0)
        mine_rows = pl.ds(pl.multiple_of(chip * ROWS, ROWS), ROWS)
        got[mine_rows, pl.ds(pl.multiple_of(p * PW, PW), PW)] = mixed(chip, p)
        return carry

    lax.fori_loop(0, PIECES, mix_piece, 0)

    load_proj.wait()

    def context_rows(i, carry):
        rows = pl.ds(pl.multiple_of(i * 256, 256), 256)
        product = lax.dot_general(
            up[rows, :], proj[...], (((1,), (1,)), ((), ())), preferred_element_type=jnp.float32
        )
        cgv[rows, :] = product.astype(jnp.bfloat16)
        return carry

    lax.fori_loop(0, TOK // 256, context_rows, 0)

    gram[...] = jnp.zeros(gram.shape, jnp.float32)

    def gram_piece(p, carry):
        def wait(k, carry):
            spread(k, p).wait_recv()
            return carry

        lax.fori_loop(1, CHIPS, wait, 0)
        part = got[:, pl.ds(pl.multiple_of(p * PW, PW), PW)]
        gram[...] += lax.dot_general(part, part, (((1,), (1,)), ((), ())), preferred_element_type=jnp.float32)
        return carry

    lax.fori_loop(0, PIECES, gram_piece, 0)
    row_at = lax.broadcasted_iota(jnp.int32, (HALF, HALF), 0)
    col_at = lax.broadcasted_iota(jnp.int32, (HALF, HALF), 1)
    same = lax.rem(row_at, ROWS) == lax.rem(col_at, ROWS)
    by_chip = jnp.sum(jnp.where(same, gram[...], 0.0).reshape(CHIPS, ROWS, HALF), axis=1)
    picks = (
        lax.div(lax.broadcasted_iota(jnp.int32, (HALF, 128), 0), ROWS)
        == lax.broadcasted_iota(jnp.int32, (HALF, 128), 1)
    ).astype(jnp.float32)
    gblock[...] = lax.dot_general(
        by_chip, picks, (((1,), (0,)), ((), ())),
        precision=lax.Precision.HIGHEST, preferred_element_type=jnp.float32,
    )
    pblock[...] = reduce_over(
        GROUP, place, lambda k: group_device(lax.rem(place + k, GROUP)), gblock, gblocks, g_send, g_recv
    )
    products = reduce_over(
        CHIPS, chip, lambda k: plane_device(plane_peer(k)), pblock, pblocks, p_send, p_recv
    )

    at_row = lax.broadcasted_iota(jnp.int32, (CHIPS, 128), 0)
    at_col = lax.broadcasted_iota(jnp.int32, (CHIPS, 128), 1)
    diagonal = at_row == at_col
    for level in range(4):
        step = 1 << level
        row_low = lax.rem(lax.div(at_row, step), 2) == 0
        col_low = lax.rem(lax.div(at_col, step), 2) == 0
        partner = at_col == jnp.where(row_low, at_row + step, at_row - step)
        norm = jnp.sum(jnp.where(diagonal, products, 0.0), axis=1, keepdims=True)
        crossed = jnp.sum(jnp.where(partner, products, 0.0), axis=1, keepdims=True)
        by = 1.0 - crossed / (2.0 * (norm + EPSILON))
        by = jnp.broadcast_to(by, (CHIPS, 128))
        weights[level] = by
        if level < 3:
            by_col = jnp.sum(jnp.where(diagonal, by, 0.0), axis=0, keepdims=True)
            products = by * products * by_col
            swapped = jnp.where(row_low, pltpu.roll(products, CHIPS - step, 0), pltpu.roll(products, step, 0))
            products = products + swapped
            swapped = jnp.where(col_low, pltpu.roll(products, 128 - step, 1), pltpu.roll(products, step, 1))
            products = products + swapped

    a = jnp.where(core == 0, x, y)
    b = jnp.where(core == 0, y, x)

    def chip_at(ra, rb):
        aa = lax.rem(a + ra, 4)
        bb = lax.rem(b + rb, 4)
        return jnp.where(core == 0, aa, bb) * 4 + jnp.where(core == 0, bb, aa)

    def shard(t, c, h):
        rows = pl.ds(pl.multiple_of((c * CHIPS + t) * ROWS, ROWS), ROWS)
        return comb.at[rows, pl.ds(pl.multiple_of(h * GW, GW), GW)]

    my_rows = pl.ds(pl.multiple_of((core * CHIPS + chip) * ROWS, ROWS), ROWS)

    def combine(i, carry):
        cols = pl.ds(pl.multiple_of(i * 128, 128), 128)

        def node(level, start):
            if level < 0:
                return got[start * ROWS : (start + 1) * ROWS, cols].astype(jnp.float32)
            half = 1 << level
            low = node(level - 1, start) * weights[level, start : start + 1, :]
            high = node(level - 1, start + half) * weights[level, start + half : start + half + 1, :]
            result = (low + high).astype(jnp.bfloat16)
            return result if level == 3 else result.astype(jnp.float32)

        comb[my_rows, cols] = node(3, 0)
        return carry

    started = []

    def relay(ra, rb, h, along, k):
        ta, tb = (k, 0) if along == "a" else (0, k)
        da, db = ((ra - k) % 4, rb) if along == "a" else (ra, (rb - k) % 4)
        ref = shard(chip_at(ra, rb), core, h)
        copy = remote(ref, ref, r_send.at[len(started)], r_recv.at[da, db, h], plane_device(chip_at(ta, tb)))
        copy.start()
        started.append(copy)

    siblings = []

    def to_sibling(ra, rb, h):
        ref = shard(chip_at(ra, rb), core, h)
        copy = remote(ref, ref, s_send.at[ra, rb, h], s_recv.at[ra, rb, h], sibling)
        copy.start()
        siblings.append(copy)

    def arrive(ra, rb, h):
        ref = shard(chip_at(ra, rb), core, h)
        remote(ref, ref, r_send.at[0], r_recv.at[ra, rb, h], sibling).wait_recv()

    def along_b(ra, h):
        relay(ra, 0, h, "b", 1)
        relay(ra, 0, h, "b", 3)

    def on_a(ra, h):
        arrive(ra, 0, h)
        if ra == 3 and h < GPIECES // 2:
            relay(3, 0, h, "a", 1)
        if ra == 1 and h >= GPIECES // 2:
            relay(1, 0, h, "a", 3)
        along_b(ra, h)
        to_sibling(ra, 0, h)

    def on_b(ra, rb, h):
        arrive(ra, rb, h)
        if rb == 3 and h < GPIECES // 2:
            relay(ra, 3, h, "b", 1)
        if rb == 1 and h >= GPIECES // 2:
            relay(ra, 1, h, "b", 3)
        to_sibling(ra, rb, h)

    for h in range(GPIECES):
        lax.fori_loop(h * (GW // 128), (h + 1) * (GW // 128), combine, 0)
        relay(0, 0, h, "a", 1)
        relay(0, 0, h, "a", 3)
        along_b(0, h)
        to_sibling(0, 0, h)
    for h in range(GPIECES):
        on_a(3, h)
        on_a(1, h)
    for h in range(GPIECES):
        on_b(0, 3, h)
        on_b(0, 1, h)
    for h in range(GPIECES):
        on_a(2, h)
    for ra in (3, 1, 2):
        for h in range(GPIECES):
            on_b(ra, 3, h)
            on_b(ra, 1, h)
    for ra in (0, 3, 1, 2):
        for h in range(GPIECES):
            arrive(ra, 2, h)
            to_sibling(ra, 2, h)

    for copy in started:
        copy.wait_send()
    for copy in siblings:
        copy.wait_send()
    for ra in range(4):
        for rb in range(4):
            for h in range(GPIECES):
                ref = shard(chip_at(rb, ra), 1 - core, h)
                remote(ref, ref, s_send.at[0, 0, 0], s_recv.at[ra, rb, h], sibling).wait_recv()

    def end_exchange(i, carry):
        exchange(i).wait_send()
        return carry

    lax.fori_loop(0, CHUNKS, end_exchange, 0)

    def end_piece(p, carry):
        def wait(k, carry):
            spread(k, p).wait_send()
            return carry

        return lax.fori_loop(1, CHIPS, wait, carry)

    lax.fori_loop(0, PIECES, end_piece, 0)


def shards(context, upstream, out_proj):
    bf16, f32 = jnp.bfloat16, jnp.float32
    vmem, dma = pltpu.VMEM, pltpu.SemaphoreType.DMA
    return pl.pallas_call(
        kernel,
        out_shape=(OUT_COMB, OUT_CG),
        in_specs=[pl.BlockSpec(memory_space=pltpu.HBM)] * 3,
        out_specs=(pl.BlockSpec(memory_space=pltpu.VMEM), pl.BlockSpec(memory_space=pltpu.VMEM)),
        scratch_shapes=[
            vmem((TOK, HALF), bf16),
            vmem((TOK, HALF), bf16),
            vmem((TOK, WIDTH), bf16),
            vmem((HEADS, WIDTH), bf16),
            vmem((HALF, TOK), bf16),
            vmem((HALF, WIDTH), bf16),
            vmem((HALF, WIDTH), bf16),
            vmem((HALF, WIDTH), bf16),
            vmem((HALF, WIDTH), bf16),
            vmem((8, 128), f32),
            vmem((GROUP, 8, 128), f32),
            vmem((HALF, HALF), f32),
            vmem((CHIPS, 128), f32),
            vmem((GROUP, CHIPS, 128), f32),
            vmem((CHIPS, 128), f32),
            vmem((CHIPS, CHIPS, 128), f32),
            vmem((4, CHIPS, 128), f32),
            dma((3,)),
            dma((CHUNKS,)),
            dma((CHUNKS,)),
            dma((CHUNKS,)),
            dma((GROUP,)),
            dma((GROUP,)),
            dma((PIECES, CHIPS)),
            dma((PIECES, CHIPS)),
            dma((GROUP,)),
            dma((GROUP,)),
            dma((CHIPS,)),
            dma((CHIPS,)),
            dma((15 * GPIECES,)),
            dma((4, 4, GPIECES)),
            dma((4, 4, GPIECES)),
            dma((4, 4, GPIECES)),
        ],
        compiler_params=pltpu.CompilerParams(
            collective_id=0, has_side_effects=True, vmem_limit_bytes=40 << 20
        ),
        cost_estimate=pl.CostEstimate(flops=8 << 30, bytes_accessed=14 << 20, transcendentals=0),
    )(context, upstream, out_proj)


OUT_COMB = jax.ShapeDtypeStruct((HEADS, WIDTH), jnp.bfloat16)
OUT_CG = jax.ShapeDtypeStruct((TOK, HEADS), jnp.bfloat16)


def solution(mesh):
    in_specs = (P("dp", "mp"), P("dp", None), P("mp", None))
    out_specs = (P("mp", None), P("dp", "mp"))
    return jax.shard_map(shards, mesh=mesh, in_specs=in_specs, out_specs=out_specs, check_vma=False)
```

time: 308 us -> 89.3 us (0.29)
  waiting for transfers between devices: 107 us -> 0 us
  Pallas kernels: 0 us -> 80.2 us
  starting transfers between devices: 62.3 us -> 0 us
  blocking collectives: 60.6 us -> 0 us
  between operations: 27.5 us -> 0.65 us
  other arithmetic: 25.3 us -> 0 us
  matrix products: 11.2 us -> 0 us
  local copies, waits for them, and re-layouts: 13.5 us -> 8.22 us
    pallas_call x0 -> x1, Pallas kernels: none -> 80.2 us  [shards(): pl.pallas_call(kernel, out_shape=(OUT_COMB, OUT_CG), in_specs=[pl.BlockSp...]
    ppermute x20 -> x0, starting transfers between devices: 62.3 us -> none  [partner_2(): lax.ppermute(value, axis, [(i, i ^ 1 << stride) for i in range(lax.axis_s...]
    psum x5 -> x0, blocking collectives: 60.6 us -> none  [shards(): sums = lax.psum(terms, 'mp')]
    ppermute x20 -> x0, waiting for transfers between devices: 59.2 us -> none  [partner_2(): lax.ppermute(value, axis, [(i, i ^ 1 << stride) for i in range(lax.axis_s...]
    all_gather x1 -> x0, waiting for transfers between devices: 47.4 us -> none  [shards(): lax.all_gather(current.reshape(row_block, width), 'dp', axis=0, tiled=True)]
    reduce_sum x5 -> x0, other arithmetic: 11.5 us -> none  [partial_terms(): jnp.sum(left_wide * right_wide)]
    dot_general x2 -> x0, matrix products: 11.2 us -> none  [the longest x1 6.62 us: shards(): lax.dot_general(upstream, out_proj, (((1,), (1,)), ((), ())), preferred_e...]
    another operation x5 -> x0, other arithmetic: 9.99 us -> none  [partial_terms(): jnp.stack([jnp.sum(left_wide * right_wide), jnp.sum(left_wide * left_wide...]
  transfers between devices with their start and end apart: 21 -> 0, of which waited for: 21 -> 0; matrix products, arithmetic and copies ran while one was open for 2% -> 0% of each run, Pallas kernels for 0% -> 0%
where the time goes in v1:
time: 89.3 us; the launch traced here: 89.1 us
  Pallas kernels  80.2 us (90%)
  local copies, waits for them, and re-layouts  8.22 us (9%)
    pallas_call x1, Pallas kernels, shards(): pl.pallas_call(kernel, out_shape=(OUT_COMB, OUT_CG), in_specs=[pl.BlockSp...  80.2 us
    unnamed x8, local copies, waits for them, and re-layouts  8.22 us

profile of v1, /device:TPU:1, one launch (start us, length us, event | category | flops | bytes accessed | tf_op | source)
XLA Modules:
  0.0 89.1 jit_solution(4214426397853163661)
XLA Ops:
  0.6 0.0 copy-start
  0.6 2.2 %copy-done = bf16[512,4096]{1,0:T(8,128)(2,1)S(1)} copy-done((bf16[512,4096]{1,0:T(8,128)(2,1)S(1)}, bf16[512,4096]{1,0:T(8,128)(2,1)}, u32[]{:S(2)}) %copy-start) | copy-done | bytes 4194328
  2.8 0.0 copy-start.1
  2.8 2.2 %copy-done.1 = bf16[512,4096]{1,0:T(8,128)(2,1)S(1)} copy-done((bf16[512,4096]{1,0:T(8,128)(2,1)S(1)}, bf16[512,4096]{1,0:T(8,128)(2,1)}, u32[]{:S(2)}) %copy-start.1) | copy-done | bytes 4194328
  5.0 0.0 copy-start.2
  5.0 1.0 %copy-done.2 = bf16[512,512]{1,0:T(8,128)(2,1)S(1)} copy-done((bf16[512,512]{1,0:T(8,128)(2,1)S(1)}, bf16[512,512]{1,0:T(8,128)(2,1)}, u32[]{:S(2)}) %copy-start.2) | copy-done | bytes 524312
  6.0 80.2 %shard_map.50 = (bf16[512,4096]{1,0:T(8,128)(2,1)S(1)}, bf16[512,512]{1,0:T(8,128)(2,1)S(1)}) custom-call(bf16[512,512]{1,0:T(8,128)(2,1)S(1)} %copy-done.2, bf16[512,4096]{1,0:T(8,128)(2,1)S(1)} %copy-done, bf16[512,4096]{1,0:T(8,128)(2,1)S(1)} %copy-done.1), custom_call_target="tpu_custom_call" | custom-call | flops 8589934592 | bytes 14680064 | tf_op jit(solution)/shard_map/pallas_call | solution.py:405
  86.3 2.0 %copy.7 = bf16[512,4096]{1,0:T(8,128)(2,1)} copy(bf16[512,4096]{1,0:T(8,128)(2,1)S(1)} %get-tuple-element.4) | data formatting | bytes 8388608
  88.3 0.8 copy.8
Async XLA Ops:
  0.6 2.2 %copy-start = (bf16[512,4096]{1,0:T(8,128)(2,1)S(1)}, bf16[512,4096]{1,0:T(8,128)(2,1)}, u32[]{:S(2)}) copy-start(bf16[512,4096]{1,0:T(8,128)(2,1)} %up_hbm.1) | copy-start | bytes 12582916
  2.8 2.2 %copy-start.1 = (bf16[512,4096]{1,0:T(8,128)(2,1)S(1)}, bf16[512,4096]{1,0:T(8,128)(2,1)}, u32[]{:S(2)}) copy-start(bf16[512,4096]{1,0:T(8,128)(2,1)} %proj_hbm.1) | copy-start | bytes 12582916
  5.0 1.0 %copy-start.2 = (bf16[512,512]{1,0:T(8,128)(2,1)S(1)}, bf16[512,512]{1,0:T(8,128)(2,1)}, u32[]{:S(2)}) copy-start(bf16[512,512]{1,0:T(8,128)(2,1)} %ctx_hbm.1) | copy-start | bytes 1572868

commit v2 on v1

--- a/solution.py
+++ b/solution.py
@@ -26,6 +26,25 @@
 GW = WIDTH // GPIECES
 
 
+def receive_semaphores():
+    index, group = {}, {}
+    for ra in range(4):
+        for rb in range(4):
+            for h in range(GPIECES):
+                if rb == 2:
+                    key = (ra, rb)
+                elif (rb == 3 and h >= GPIECES // 2) or (rb == 1 and h < GPIECES // 2):
+                    key = (ra, rb, "rest")
+                else:
+                    key = (ra, rb, h)
+                if (ra, rb) != (0, 0):
+                    index[ra, rb, h] = group.setdefault(key, len(group))
+    return index, len(group)
+
+
+RECV, N_RECV = receive_semaphores()
+
+
 def remote(src, dst, send, recv, device):
     return pltpu.make_async_remote_copy(
         src_ref=src, dst_ref=dst, send_sem=send, recv_sem=recv, device_id=device, device_id_type=MESH
@@ -69,7 +88,7 @@
 
     def load_up(i):
         cols = pl.ds(pl.multiple_of(i * CW, CW), CW)
-        return pltpu.make_async_copy(up_hbm.at[:, cols], up.at[:, cols], up_sem.at[i])
+        return pltpu.make_async_copy(up_hbm.at[:, cols], up.at[:, cols], up_sem)
 
     for i in range(CHUNKS):
         load_up(i).start()
@@ -101,14 +120,13 @@
 
     load_sib.wait()
     left_t[...] = ctx_sib[...].T
-    for i in range(CHUNKS):
-        load_up(i).wait()
+    pltpu.make_async_copy(up_hbm, up, up_sem).wait()
     lax.fori_loop(0, CHUNKS, gradient(sent), 0)
     pl.semaphore_wait(barrier, GROUP - 1 + CHIPS - 1)
 
     def exchange(i):
         cols = pl.ds(pl.multiple_of(i * CW, CW), CW)
-        return remote(sent.at[:, cols], par.at[:, cols], x_send.at[i], x_recv.at[i], sibling)
+        return remote(sent.at[:, cols], par.at[:, cols], x_send, x_recv.at[i], sibling)
 
     def start_exchange(i, carry):
         exchange(i).start()
@@ -155,19 +173,13 @@
     def reduce_over(count, me, peer, src, dst, send, recv):
         dst[me] = src[...]
 
-        def copy(k):
-            return remote(src, dst.at[me], send.at[k], recv.at[k], peer(k))
-
         def start(k, carry):
-            copy(k).start()
+            remote(src, dst.at[me], send, recv, peer(k)).start()
             return carry
 
-        def wait(k, carry):
-            copy(k).wait()
-            return carry
-
         lax.fori_loop(1, count, start, 0)
-        lax.fori_loop(1, count, wait, 0)
+        others = dst.at[pl.ds(0, count - 1)]
+        remote(others, others, send, recv, sibling).wait()
         total = dst[0]
         for i in range(1, count):
             total = total + dst[i]
@@ -195,7 +207,7 @@
         rows = pl.ds(pl.multiple_of(t * ROWS, ROWS), ROWS)
         to = pl.ds(pl.multiple_of(chip * ROWS, ROWS), ROWS)
         cols = pl.ds(pl.multiple_of(p * PW, PW), PW)
-        return remote(own.at[rows, cols], got.at[to, cols], a_send.at[p, k], a_recv.at[p, k], plane_device(t))
+        return remote(own.at[rows, cols], got.at[to, cols], a_send, a_recv.at[p], plane_device(t))
 
     def mix_piece(p, carry):
         def mix_one(k, carry):
@@ -228,11 +240,8 @@
     gram[...] = jnp.zeros(gram.shape, jnp.float32)
 
     def gram_piece(p, carry):
-        def wait(k, carry):
-            spread(k, p).wait_recv()
-            return carry
-
-        lax.fori_loop(1, CHIPS, wait, 0)
+        others = got.at[pl.ds(0, HALF - ROWS), pl.ds(pl.multiple_of(p * PW, PW), PW)]
+        remote(others, others, a_send, a_recv.at[p], sibling).wait_recv()
         part = got[:, pl.ds(pl.multiple_of(p * PW, PW), PW)]
         gram[...] += lax.dot_general(part, part, (((1,), (1,)), ((), ())), preferred_element_type=jnp.float32)
         return carry
@@ -246,19 +255,22 @@
         lax.div(lax.broadcasted_iota(jnp.int32, (HALF, 128), 0), ROWS)
         == lax.broadcasted_iota(jnp.int32, (HALF, 128), 1)
     ).astype(jnp.float32)
-    gblock[...] = lax.dot_general(
+    products = lax.dot_general(
         by_chip, picks, (((1,), (0,)), ((), ())),
         precision=lax.Precision.HIGHEST, preferred_element_type=jnp.float32,
     )
+    gblock[...] = products[:8] + pltpu.roll(products[8:], CHIPS, 1)
     pblock[...] = reduce_over(
         GROUP, place, lambda k: group_device(lax.rem(place + k, GROUP)), gblock, gblocks, g_send, g_recv
     )
-    products = reduce_over(
+    packed = reduce_over(
         CHIPS, chip, lambda k: plane_device(plane_peer(k)), pblock, pblocks, p_send, p_recv
     )
 
     at_row = lax.broadcasted_iota(jnp.int32, (CHIPS, 128), 0)
     at_col = lax.broadcasted_iota(jnp.int32, (CHIPS, 128), 1)
+    products = jnp.concatenate([packed, pltpu.roll(packed, 128 - CHIPS, 1)], axis=0)
+    products = jnp.where(at_col < CHIPS, products, 0.0)
     diagonal = at_row == at_col
     for level in range(4):
         step = 1 << level
@@ -286,9 +298,9 @@
         bb = lax.rem(b + rb, 4)
         return jnp.where(core == 0, aa, bb) * 4 + jnp.where(core == 0, bb, aa)
 
-    def shard(t, c, h):
+    def shard(t, c, h, count=1):
         rows = pl.ds(pl.multiple_of((c * CHIPS + t) * ROWS, ROWS), ROWS)
-        return comb.at[rows, pl.ds(pl.multiple_of(h * GW, GW), GW)]
+        return comb.at[rows, pl.ds(h * GW, count * GW)]
 
     my_rows = pl.ds(pl.multiple_of((core * CHIPS + chip) * ROWS, ROWS), ROWS)
 
@@ -307,27 +319,19 @@
         comb[my_rows, cols] = node(3, 0)
         return carry
 
-    started = []
-
     def relay(ra, rb, h, along, k):
         ta, tb = (k, 0) if along == "a" else (0, k)
         da, db = ((ra - k) % 4, rb) if along == "a" else (ra, (rb - k) % 4)
         ref = shard(chip_at(ra, rb), core, h)
-        copy = remote(ref, ref, r_send.at[len(started)], r_recv.at[da, db, h], plane_device(chip_at(ta, tb)))
-        copy.start()
-        started.append(copy)
-
-    siblings = []
-
-    def to_sibling(ra, rb, h):
-        ref = shard(chip_at(ra, rb), core, h)
-        copy = remote(ref, ref, s_send.at[ra, rb, h], s_recv.at[ra, rb, h], sibling)
-        copy.start()
-        siblings.append(copy)
-
-    def arrive(ra, rb, h):
-        ref = shard(chip_at(ra, rb), core, h)
-        remote(ref, ref, r_send.at[0], r_recv.at[ra, rb, h], sibling).wait_recv()
+        remote(ref, ref, r_send, r_recv.at[RECV[da, db, h]], plane_device(chip_at(ta, tb))).start()
+
+    def to_sibling(ra, rb, h, count=1):
+        ref = shard(chip_at(ra, rb), core, h, count)
+        remote(ref, ref, s_send, s_recv, sibling).start()
+
+    def arrive(ra, rb, h, count=1):
+        ref = shard(chip_at(ra, rb), core, h, count)
+        remote(ref, ref, r_send, r_recv.at[RECV[ra, rb, h]], sibling).wait_recv()
 
     def along_b(ra, h):
         relay(ra, 0, h, "b", 1)
@@ -342,67 +346,75 @@
         along_b(ra, h)
         to_sibling(ra, 0, h)
 
-    def on_b(ra, rb, h):
-        arrive(ra, rb, h)
-        if rb == 3 and h < GPIECES // 2:
-            relay(ra, 3, h, "b", 1)
-        if rb == 1 and h >= GPIECES // 2:
-            relay(ra, 1, h, "b", 3)
-        to_sibling(ra, rb, h)
+    HB = GPIECES // 2
+
+    def relayed(ra, h):
+        arrive(ra, 3, h)
+        relay(ra, 3, h, "b", 1)
+        arrive(ra, 1, h + HB)
+        relay(ra, 1, h + HB, "b", 3)
+
+    def ended(ra):
+        to_sibling(ra, 3, 0, HB)
+        to_sibling(ra, 1, HB, HB)
+        arrive(ra, 3, HB, HB)
+        to_sibling(ra, 3, HB, HB)
+        arrive(ra, 1, 0, HB)
+        to_sibling(ra, 1, 0, HB)
 
     for h in range(GPIECES):
         lax.fori_loop(h * (GW // 128), (h + 1) * (GW // 128), combine, 0)
         relay(0, 0, h, "a", 1)
         relay(0, 0, h, "a", 3)
         along_b(0, h)
-        to_sibling(0, 0, h)
+    to_sibling(0, 0, 0, GPIECES)
     for h in range(GPIECES):
         on_a(3, h)
         on_a(1, h)
-    for h in range(GPIECES):
-        on_b(0, 3, h)
-        on_b(0, 1, h)
+    for h in range(HB):
+        relayed(0, h)
     for h in range(GPIECES):
         on_a(2, h)
     for ra in (3, 1, 2):
-        for h in range(GPIECES):
-            on_b(ra, 3, h)
-            on_b(ra, 1, h)
+        for h in range(HB):
+            relayed(ra, h)
     for ra in (0, 3, 1, 2):
-        for h in range(GPIECES):
-            arrive(ra, 2, h)
-            to_sibling(ra, 2, h)
-
-    for copy in started:
-        copy.wait_send()
-    for copy in siblings:
-        copy.wait_send()
-    for ra in range(4):
-        for rb in range(4):
-            for h in range(GPIECES):
-                ref = shard(chip_at(rb, ra), 1 - core, h)
-                remote(ref, ref, s_send.at[0, 0, 0], s_recv.at[ra, rb, h], sibling).wait_recv()
-
-    def end_exchange(i, carry):
-        exchange(i).wait_send()
-        return carry
-
-    lax.fori_loop(0, CHUNKS, end_exchange, 0)
-
-    def end_piece(p, carry):
-        def wait(k, carry):
-            spread(k, p).wait_send()
-            return carry
-
-        return lax.fori_loop(1, CHIPS, wait, carry)
-
-    lax.fori_loop(0, PIECES, end_piece, 0)
+        ended(ra)
+    for ra in (0, 3, 1, 2):
+        arrive(ra, 2, 0, GPIECES)
+        to_sibling(ra, 2, 0, GPIECES)
+
+    mine = comb.at[pl.ds(0, HALF - ROWS)]
+    remote(mine, mine, r_send, r_recv.at[0], sibling).wait_send()
+    theirs = comb.at[pl.ds(0, HALF)]
+    remote(theirs, theirs, s_send, s_recv, sibling).wait()
+    remote(sent, par, x_send, x_recv.at[0], sibling).wait_send()
+
+    others = got.at[pl.ds(0, HALF - ROWS)]
+    remote(others, others, a_send, a_recv.at[0], sibling).wait_send()
+
+
+OUT_PARTS = 4
+
+
+def store(comb, cgv, comb_hbm, cg_hbm, sems):
+    copies = [pltpu.make_async_copy(cgv, cg_hbm, sems.at[OUT_PARTS])]
+    for i in range(OUT_PARTS):
+        rows = pl.ds(i * (HEADS // OUT_PARTS), HEADS // OUT_PARTS)
+        copies.append(pltpu.make_async_copy(comb.at[rows], comb_hbm.at[rows], sems.at[i]))
+    for copy in copies:
+        copy.start()
+    for copy in copies:
+        copy.wait()
 
 
 def shards(context, upstream, out_proj):
+    context, upstream, out_proj = (
+        pltpu.with_memory_space_constraint(v, pltpu.HBM) for v in (context, upstream, out_proj)
+    )
     bf16, f32 = jnp.bfloat16, jnp.float32
     vmem, dma = pltpu.VMEM, pltpu.SemaphoreType.DMA
-    return pl.pallas_call(
+    results = pl.pallas_call(
         kernel,
         out_shape=(OUT_COMB, OUT_CG),
         in_specs=[pl.BlockSpec(memory_space=pltpu.HBM)] * 3,
@@ -420,33 +432,41 @@
             vmem((8, 128), f32),
             vmem((GROUP, 8, 128), f32),
             vmem((HALF, HALF), f32),
-            vmem((CHIPS, 128), f32),
-            vmem((GROUP, CHIPS, 128), f32),
-            vmem((CHIPS, 128), f32),
-            vmem((CHIPS, CHIPS, 128), f32),
+            vmem((8, 128), f32),
+            vmem((GROUP, 8, 128), f32),
+            vmem((8, 128), f32),
+            vmem((CHIPS, 8, 128), f32),
             vmem((4, CHIPS, 128), f32),
             dma((3,)),
+            dma,
+            dma,
             dma((CHUNKS,)),
-            dma((CHUNKS,)),
-            dma((CHUNKS,)),
-            dma((GROUP,)),
-            dma((GROUP,)),
-            dma((PIECES, CHIPS)),
-            dma((PIECES, CHIPS)),
-            dma((GROUP,)),
-            dma((GROUP,)),
-            dma((CHIPS,)),
-            dma((CHIPS,)),
-            dma((15 * GPIECES,)),
-            dma((4, 4, GPIECES)),
-            dma((4, 4, GPIECES)),
-            dma((4, 4, GPIECES)),
+            dma,
+            dma,
+            dma,
+            dma((PIECES,)),
+            dma,
+            dma,
+            dma,
+            dma,
+            dma,
+            dma((N_RECV,)),
+            dma,
+            dma,
         ],
         compiler_params=pltpu.CompilerParams(
             collective_id=0, has_side_effects=True, vmem_limit_bytes=40 << 20
         ),
         cost_estimate=pl.CostEstimate(flops=8 << 30, bytes_accessed=14 << 20, transcendentals=0),
     )(context, upstream, out_proj)
+    return pl.pallas_call(
+        store,
+        out_shape=(OUT_COMB, OUT_CG),
+        in_specs=[pl.BlockSpec(memory_space=pl.ANY)] * 2,
+        out_specs=[pl.BlockSpec(memory_space=pltpu.HBM)] * 2,
+        compiler_params=pltpu.CompilerParams(vmem_limit_bytes=1 << 20),
+        scratch_shapes=[pltpu.SemaphoreType.DMA((OUT_PARTS + 1,))],
+    )(*results)
 
 
 OUT_COMB = jax.ShapeDtypeStruct((HEADS, WIDTH), jnp.bfloat16)

time: 89.3 us -> 78.1 us (0.87)
  local copies, waits for them, and re-layouts: 8.22 us -> 0 us
  Pallas kernels: 80.2 us -> 77.3 us
    unnamed x8 -> x0, local copies, waits for them, and re-layouts: 8.22 us -> none
    pallas_call x1, Pallas kernels: 80.2 us -> 75.1 us  [shards(): pl.pallas_call(kernel, out_shape=(OUT_COMB, OUT_CG), in_specs=[pl.BlockSp...]
    pallas_call x0 -> x1, Pallas kernels: none -> 2.22 us  [shards(): pl.pallas_call(store, out_shape=(OUT_COMB, OUT_CG), in_specs=[pl.BlockSpe...]
where the time goes in v2:
time: 78.1 us; the launch traced here: 78 us
  Pallas kernels  77.3 us (99%)
    pallas_call x1, Pallas kernels, shards(): pl.pallas_call(kernel, out_shape=(OUT_COMB, OUT_CG), in_specs=[pl.BlockSp...  75.1 us
    pallas_call x1, Pallas kernels, shards(): pl.pallas_call(store, out_shape=(OUT_COMB, OUT_CG), in_specs=[pl.BlockSpe...  2.22 us

profile of v2, /device:TPU:1, one launch (start us, length us, event | category | flops | bytes accessed | tf_op | source)
XLA Modules:
  0.0 78.0 jit_solution(8291990321420628393)
XLA Ops:
  0.6 75.1 %shard_map.50 = (bf16[512,4096]{1,0:T(8,128)(2,1)S(1)}, bf16[512,512]{1,0:T(8,128)(2,1)S(1)}) custom-call(bf16[512,512]{1,0:T(8,128)(2,1)} %ctx_hbm.1, bf16[512,4096]{1,0:T(8,128)(2,1)} %up_hbm.1, bf16[512,4096]{1,0:T(8,128)(2,1)} %proj_hbm.1), custom_call_target="tpu_custom_call" | custom-call | flops 8589934592 | bytes 14680064 | tf_op jit(solution)/shard_map/pallas_call | solution.py:417
  75.8 2.2 %shard_map.51 = (bf16[512,4096]{1,0:T(8,128)(2,1)}, bf16[512,512]{1,0:T(8,128)(2,1)}) custom-call(bf16[512,4096]{1,0:T(8,128)(2,1)S(1)} %get-tuple-element.4.comb, bf16[512,512]{1,0:T(8,128)(2,1)S(1)} %get-tuple-element.5.cgv), custom_call_target="tpu_custom_call" | custom-call | tf_op jit(solution)/shard_map/pallas_call | solution.py:462

commit v3 on v2

--- a/solution.py
+++ b/solution.py
@@ -20,8 +20,13 @@
 WIDTH = 4096
 CHUNKS = 8
 CW = WIDTH // CHUNKS
-PIECES = 4
+PIECES = 16
 PW = WIDTH // PIECES
+EARLY = 1
+FIRSTP = 2
+RAWP = 3
+FIRST = FIRSTP * PW
+RAW = RAWP * PW
 GPIECES = 4
 GW = WIDTH // GPIECES
 
@@ -54,9 +59,9 @@
 def kernel(
     ctx_hbm, up_hbm, proj_hbm, comb, cgv,
     ctx_own, ctx_sib, up, proj, left_t, sent, own, par, got,
-    block, blocks, gram, gblock, gblocks, pblock, pblocks, weights,
+    raw, factor, factors, block, blocks, gram, gblock, gblocks, pblock, pblocks, weights,
     load_sem, up_sem, x_send, x_recv, z_send, z_recv, a_send, a_recv,
-    g_send, g_recv, p_send, p_recv, r_send, r_recv, s_send, s_recv,
+    w_send, w_recv, f_send, f_recv, g_send, g_recv, p_send, p_recv, r_send, r_recv, s_send, s_recv,
 ):
     dp = lax.axis_index("dp")
     z = lax.axis_index("mp")
@@ -122,6 +127,9 @@
     left_t[...] = ctx_sib[...].T
     pltpu.make_async_copy(up_hbm, up, up_sem).wait()
     lax.fori_loop(0, CHUNKS, gradient(sent), 0)
+    load_own.wait()
+    left_t[...] = ctx_own[...].T
+    lax.fori_loop(0, EARLY, gradient(own), 0)
     pl.semaphore_wait(barrier, GROUP - 1 + CHIPS - 1)
 
     def exchange(i):
@@ -133,9 +141,25 @@
         return carry
 
     lax.fori_loop(0, CHUNKS, start_exchange, 0)
-    load_own.wait()
-    left_t[...] = ctx_own[...].T
-    lax.fori_loop(0, CHUNKS, gradient(own), 0)
+
+    def spread_raw(values, replica, begin, end):
+        def start(k, carry):
+            t = plane_peer(k)
+            rows = pl.ds(pl.multiple_of(t * ROWS, ROWS), ROWS)
+            to = pl.ds(pl.multiple_of(chip * ROWS, ROWS), ROWS)
+            remote(
+                values.at[rows, pl.ds(begin, end - begin)],
+                raw.at[replica, to, pl.ds(begin, end - begin)],
+                w_send, w_recv, plane_device(t),
+            ).start()
+            return carry
+
+        if end > begin:
+            lax.fori_loop(1, CHIPS, start, 0)
+
+    lax.fori_loop(EARLY, max(FIRST // CW, EARLY), gradient(own), 0)
+    spread_raw(own, core, 0, FIRST)
+    lax.fori_loop(max(FIRST // CW, EARLY), CHUNKS, gradient(own), 0)
 
     zero = jnp.zeros((8, CW), jnp.float32)
 
@@ -156,21 +180,21 @@
 
         return lax.fori_loop(0, HALF // 16, rows_sums, sums, unroll=2)
 
-    crossed, mine, theirs = lax.fori_loop(0, CHUNKS, chunk_sums, (zero, zero, zero))
-
-    def to_row(v):
-        v = jnp.sum(v, axis=0, keepdims=True)
-        return sum(v[:, j * 128 : (j + 1) * 128] for j in range(CW // 128))
-
-    crossed, mine, theirs = to_row(crossed), to_row(mine), to_row(theirs)
+    sums = lax.fori_loop(0, FIRST // CW, chunk_sums, (zero, zero, zero))
+    spread_raw(par, 1 - core, 0, FIRST)
+    crossed, mine, theirs = lax.fori_loop(FIRST // CW, CHUNKS, chunk_sums, sums)
+
+    lane = lax.broadcasted_iota(jnp.int32, (1, 128), 1)
+
+    def total_of(v):
+        return jnp.sum(jnp.sum(v, axis=0, keepdims=True), axis=1, keepdims=True)
+
+    crossed, mine, theirs = total_of(crossed), total_of(mine), total_of(theirs)
     first = jnp.where(core == 0, mine, theirs)
     second = jnp.where(core == 0, theirs, mine)
-    block[...] = jnp.zeros((8, 128), jnp.float32)
-    block[0:1, :] = crossed
-    block[1:2, :] = first
-    block[2:3, :] = second
-
-    def reduce_over(count, me, peer, src, dst, send, recv):
+    block[...] = jnp.where(lane == 0, crossed, jnp.where(lane == 1, first, jnp.where(lane == 2, second, 0.0)))
+
+    def reduce_over(count, me, peer, src, dst, send, recv, meanwhile=lambda: None):
         dst[me] = src[...]
 
         def start(k, carry):
@@ -178,6 +202,7 @@
             return carry
 
         lax.fori_loop(1, count, start, 0)
+        meanwhile()
         others = dst.at[pl.ds(0, count - 1)]
         remote(others, others, send, recv, sibling).wait()
         total = dst[0]
@@ -185,15 +210,30 @@
             total = total + dst[i]
         return total
 
+    def more_raw():
+        spread_raw(own, core, FIRST, RAW)
+        spread_raw(par, 1 - core, FIRST, RAW)
+
     total = reduce_over(
-        GROUP, place, lambda k: group_device(lax.rem(place + k, GROUP)), block, blocks, z_send, z_recv
-    )
-    total = jnp.sum(total, axis=1, keepdims=True)
-    crossed, first, second = total[0:1], total[1:2], total[2:3]
+        GROUP, place, lambda k: group_device(lax.rem(place + k, GROUP)), block, blocks, z_send, z_recv, more_raw
+    )
+    crossed, first, second = (
+        jnp.sum(jnp.where(lane == i, total, 0.0), axis=1, keepdims=True) for i in range(3)
+    )
     first_by = 1.0 - crossed / (2.0 * (first + EPSILON))
     second_by = 1.0 - crossed / (2.0 * (second + EPSILON))
     own_by = jnp.where(core == 0, first_by, second_by)
     par_by = jnp.where(core == 0, second_by, first_by)
+
+    if RAWP:
+        factor[0:1, :] = jnp.broadcast_to(first_by, (1, 128))
+        factor[1:2, :] = jnp.broadcast_to(second_by, (1, 128))
+
+        def send_factor(k, carry):
+            remote(factor, factors.at[chip], f_send, f_recv, plane_device(plane_peer(k))).start()
+            return carry
+
+        lax.fori_loop(1, CHIPS, send_factor, 0)
 
     def mixed(t, p):
         rows = pl.ds(pl.multiple_of(t * ROWS, ROWS), ROWS)
@@ -223,7 +263,31 @@
         got[mine_rows, pl.ds(pl.multiple_of(p * PW, PW), PW)] = mixed(chip, p)
         return carry
 
-    lax.fori_loop(0, PIECES, mix_piece, 0)
+    lax.fori_loop(RAWP, PIECES, mix_piece, 0)
+
+    if RAWP:
+        others = raw.at[:, pl.ds(0, HALF - ROWS)]
+        remote(others, others, w_send, w_recv, sibling).wait()
+        others = factors.at[pl.ds(0, CHIPS - 1)]
+        remote(others, others, f_send, f_recv, sibling).wait()
+
+        def mix_raw(k, carry):
+            t = plane_peer(k)
+            rows = pl.ds(pl.multiple_of(t * ROWS, ROWS), ROWS)
+            by = factors[t]
+            left = raw[0, rows, :].astype(jnp.float32)
+            right = raw[1, rows, :].astype(jnp.float32)
+            got[rows, pl.ds(0, RAW)] = (by[0:1, 0:1] * left + by[1:2, 0:1] * right).astype(jnp.bfloat16)
+            return carry
+
+        lax.fori_loop(1, CHIPS, mix_raw, 0)
+
+        def mix_own(p, carry):
+            mine_rows = pl.ds(pl.multiple_of(chip * ROWS, ROWS), ROWS)
+            got[mine_rows, pl.ds(pl.multiple_of(p * PW, PW), PW)] = mixed(chip, p)
+            return carry
+
+        lax.fori_loop(0, RAWP, mix_own, 0)
 
     load_proj.wait()
 
@@ -240,8 +304,11 @@
     gram[...] = jnp.zeros(gram.shape, jnp.float32)
 
     def gram_piece(p, carry):
-        others = got.at[pl.ds(0, HALF - ROWS), pl.ds(pl.multiple_of(p * PW, PW), PW)]
-        remote(others, others, a_send, a_recv.at[p], sibling).wait_recv()
+        @pl.when(p >= RAWP)
+        def _():
+            others = got.at[pl.ds(0, HALF - ROWS), pl.ds(pl.multiple_of(p * PW, PW), PW)]
+            remote(others, others, a_send, a_recv.at[p], sibling).wait_recv()
+
         part = got[:, pl.ds(pl.multiple_of(p * PW, PW), PW)]
         gram[...] += lax.dot_general(part, part, (((1,), (1,)), ((), ())), preferred_element_type=jnp.float32)
         return carry
@@ -253,13 +320,18 @@
     by_chip = jnp.sum(jnp.where(same, gram[...], 0.0).reshape(CHIPS, ROWS, HALF), axis=1)
     picks = (
         lax.div(lax.broadcasted_iota(jnp.int32, (HALF, 128), 0), ROWS)
-        == lax.broadcasted_iota(jnp.int32, (HALF, 128), 1)
+        == lax.rem(lax.broadcasted_iota(jnp.int32, (HALF, 128), 1), CHIPS)
     ).astype(jnp.float32)
     products = lax.dot_general(
         by_chip, picks, (((1,), (0,)), ((), ())),
         precision=lax.Precision.HIGHEST, preferred_element_type=jnp.float32,
     )
-    gblock[...] = products[:8] + pltpu.roll(products[8:], CHIPS, 1)
+    at_row = lax.broadcasted_iota(jnp.int32, (CHIPS, 128), 0)
+    at_col = lax.broadcasted_iota(jnp.int32, (CHIPS, 128), 1)
+    in_group = lax.div(at_col, CHIPS) == lax.rem(at_row, 8)
+    products = jnp.where(in_group, products, 0.0)
+    gblock[0:1, :] = jnp.sum(products[:8], axis=0, keepdims=True)
+    gblock[1:2, :] = jnp.sum(products[8:], axis=0, keepdims=True)
     pblock[...] = reduce_over(
         GROUP, place, lambda k: group_device(lax.rem(place + k, GROUP)), gblock, gblocks, g_send, g_recv
     )
@@ -267,9 +339,12 @@
         CHIPS, chip, lambda k: plane_device(plane_peer(k)), pblock, pblocks, p_send, p_recv
     )
 
-    at_row = lax.broadcasted_iota(jnp.int32, (CHIPS, 128), 0)
-    at_col = lax.broadcasted_iota(jnp.int32, (CHIPS, 128), 1)
-    products = jnp.concatenate([packed, pltpu.roll(packed, 128 - CHIPS, 1)], axis=0)
+    products = jnp.concatenate(
+        [jnp.broadcast_to(packed[0:1], (8, 128)), jnp.broadcast_to(packed[1:2], (8, 128))], axis=0
+    )
+    products = jnp.where(in_group, products, 0.0)
+    for shift in (16, 32, 64):
+        products = products + pltpu.roll(products, shift, 1)
     products = jnp.where(at_col < CHIPS, products, 0.0)
     diagonal = at_row == at_col
     for level in range(4):
@@ -390,7 +465,7 @@
     remote(theirs, theirs, s_send, s_recv, sibling).wait()
     remote(sent, par, x_send, x_recv.at[0], sibling).wait_send()
 
-    others = got.at[pl.ds(0, HALF - ROWS)]
+    others = got.at[pl.ds(0, HALF - ROWS), pl.ds(RAW, WIDTH - RAW)]
     remote(others, others, a_send, a_recv.at[0], sibling).wait_send()
 
 
@@ -429,13 +504,16 @@
             vmem((HALF, WIDTH), bf16),
             vmem((HALF, WIDTH), bf16),
             vmem((HALF, WIDTH), bf16),
-            vmem((8, 128), f32),
-            vmem((GROUP, 8, 128), f32),
-            vmem((HALF, HALF), f32),
-            vmem((8, 128), f32),
-            vmem((GROUP, 8, 128), f32),
+            vmem((2, HALF, max(RAW, 128)), bf16),
             vmem((8, 128), f32),
             vmem((CHIPS, 8, 128), f32),
+            vmem((1, 128), f32),
+            vmem((GROUP, 1, 128), f32),
+            vmem((HALF, HALF), f32),
+            vmem((2, 128), f32),
+            vmem((GROUP, 2, 128), f32),
+            vmem((2, 128), f32),
+            vmem((CHIPS, 2, 128), f32),
             vmem((4, CHIPS, 128), f32),
             dma((3,)),
             dma,
@@ -445,6 +523,10 @@
             dma,
             dma,
             dma((PIECES,)),
+            dma,
+            dma,
+            dma,
+            dma,
             dma,
             dma,
             dma,

time: 78.1 us -> 74.7 us (0.956)
  Pallas kernels: 77.3 us -> 74 us
    pallas_call x1, Pallas kernels: 75.1 us -> 71.8 us  [shards(): pl.pallas_call(kernel, out_shape=(OUT_COMB, OUT_CG), in_specs=[pl.BlockSp...]
where the time goes in v3:
time: 74.7 us; the launch traced here: 74.6 us
  Pallas kernels  74 us (99%)
    pallas_call x1, Pallas kernels, shards(): pl.pallas_call(kernel, out_shape=(OUT_COMB, OUT_CG), in_specs=[pl.BlockSp...  71.8 us
    pallas_call x1, Pallas kernels, shards(): pl.pallas_call(store, out_shape=(OUT_COMB, OUT_CG), in_specs=[pl.BlockSpe...  2.22 us

profile of v3, /device:TPU:1, one launch (start us, length us, event | category | flops | bytes accessed | tf_op | source)
XLA Modules:
  0.0 74.6 jit_solution(10578311352177773315)
XLA Ops:
  0.6 71.8 %shard_map.50 = (bf16[512,4096]{1,0:T(8,128)(2,1)S(1)}, bf16[512,512]{1,0:T(8,128)(2,1)S(1)}) custom-call(bf16[512,512]{1,0:T(8,128)(2,1)} %ctx_hbm.1, bf16[512,4096]{1,0:T(8,128)(2,1)} %up_hbm.1, bf16[512,4096]{1,0:T(8,128)(2,1)} %proj_hbm.1), custom_call_target="tpu_custom_call" | custom-call | flops 8589934592 | bytes 14680064 | tf_op jit(solution)/shard_map/pallas_call | solution.py:492
  72.4 2.2 %shard_map.51 = (bf16[512,4096]{1,0:T(8,128)(2,1)}, bf16[512,512]{1,0:T(8,128)(2,1)}) custom-call(bf16[512,4096]{1,0:T(8,128)(2,1)S(1)} %get-tuple-element.4.comb, bf16[512,512]{1,0:T(8,128)(2,1)S(1)} %get-tuple-element.5.cgv), custom_call_target="tpu_custom_call" | custom-call | tf_op jit(solution)/shard_map/pallas_call | solution.py:544

commit v4 on v3

--- a/solution.py
+++ b/solution.py
@@ -178,7 +178,7 @@
 
             return crossed + fold(a * b), mine + fold(a * a), theirs + fold(b * b)
 
-        return lax.fori_loop(0, HALF // 16, rows_sums, sums, unroll=2)
+        return lax.fori_loop(0, HALF // 16, rows_sums, sums, unroll=8)
 
     sums = lax.fori_loop(0, FIRST // CW, chunk_sums, (zero, zero, zero))
     spread_raw(par, 1 - core, 0, FIRST)

time: 74.7 us -> 74.7 us (level)
  no operation moved by 1% of the time
where the time goes in v4:
time: 74.7 us; the launch traced here: 74.6 us
  Pallas kernels  74 us (99%)
    pallas_call x1, Pallas kernels, shards(): pl.pallas_call(kernel, out_shape=(OUT_COMB, OUT_CG), in_specs=[pl.BlockSp...  71.8 us
    pallas_call x1, Pallas kernels, shards(): pl.pallas_call(store, out_shape=(OUT_COMB, OUT_CG), in_specs=[pl.BlockSpe...  2.22 us

profile of v4, /device:TPU:1, one launch (start us, length us, event | category | flops | bytes accessed | tf_op | source)
XLA Modules:
  0.0 74.6 jit_solution(18221778418074010439)
XLA Ops:
  0.6 71.8 %shard_map.50 = (bf16[512,4096]{1,0:T(8,128)(2,1)S(1)}, bf16[512,512]{1,0:T(8,128)(2,1)S(1)}) custom-call(bf16[512,512]{1,0:T(8,128)(2,1)} %ctx_hbm.1, bf16[512,4096]{1,0:T(8,128)(2,1)} %up_hbm.1, bf16[512,4096]{1,0:T(8,128)(2,1)} %proj_hbm.1), custom_call_target="tpu_custom_call" | custom-call | flops 8589934592 | bytes 14680064 | tf_op jit(solution)/shard_map/pallas_call | solution.py:492
  72.4 2.2 %shard_map.51 = (bf16[512,4096]{1,0:T(8,128)(2,1)}, bf16[512,512]{1,0:T(8,128)(2,1)}) custom-call(bf16[512,4096]{1,0:T(8,128)(2,1)S(1)} %get-tuple-element.4.comb, bf16[512,512]{1,0:T(8,128)(2,1)S(1)} %get-tuple-element.5.cgv), custom_call_target="tpu_custom_call" | custom-call | tf_op jit(solution)/shard_map/pallas_call | solution.py:544
